TPU v7x, 32 devices: a whole 2x2x4 slice. The times are simulated.
32 devices in a mesh: inst: 2 (over y), ax: 8 (over z, core), circ: 2 (over x).
Axes of the slice: x: 2, y: 2, z: 4, core: 2. Of those that a mesh axis runs over, the one named last changes fastest.
Arguments:
- flow_state: float32 [2, 7, 64, 128, 128], P('inst', None, 'ax', 'circ'), may hold values from -2 to 40, as said below
- thinc_flags: int32 [2, 64, 128], P('inst', 'ax', 'circ'), may hold values 0 or 1
Outputs:
- new_state: float32 [2, 7, 64, 128, 128], P('inst', None, 'ax', 'circ')
Inputs may be any that keep to these rules, and one draw needn't show every extreme that they name: `flow_state`: every cell holds a two-phase state with positive partial densities and positive pressure, whose seventh field, the volume fraction, lies between 0.02 and 0.98.
All inputs are finite; a program needn't handle non-finite values. No bound on the sum of `thinc_flags` on one device may be relied on, other than what follows from the above.
Results may differ from a plain program's by a relative error of at most 0.0003.
Values sent between devices are 32-bit elements; how exact they have to be, the bound alone decides.
A program may use at most 64 MiB of HBM per device.

v0:
```python
import jax
import jax.numpy as jnp
from jax import lax
from jax.sharding import PartitionSpec as P

G_LIQ = 4.4
P_LIQ = 6.0
G_GAS = 1.4
BETA = 1.6
EPSA = 0.1
ALPHA = 4.0
DIAG0 = 0.016
OMEGA = 1.0
NU_T = 0.25


def extended(block, sides, width):
    for axis, dim in sides:
        count = lax.axis_size(axis)
        forward = [(i, i + 1) for i in range(count - 1)]
        forward.append((count - 1, 0))
        backward = [(target, source) for source, target in forward]
        low = lax.ppermute(
            lax.slice_in_dim(block, block.shape[dim] - width, None, axis=dim), axis, forward
        )
        high = lax.ppermute(lax.slice_in_dim(block, 0, width, axis=dim), axis, backward)
        block = jnp.concatenate([low, block, high], axis=dim)
    return block


def shifted(block, axis, distance):
    devices = range(lax.axis_size(axis))
    route = [((i - distance) % len(devices), i) for i in devices]
    return lax.ppermute(block, axis, route)


def from_behind(value, axis, by):
    devices = lax.axis_size(axis)
    pairs = [(i, i + by) for i in range(devices) if 0 <= i + by < devices]
    return lax.ppermute(value, axis, pairs)


def spectral_table(period_count):
    harmonic = jnp.arange(period_count, dtype=jnp.int32)
    phase_angle = jnp.pi / period_count * harmonic.astype(jnp.float32)
    sine_safe = jnp.where(harmonic == 0, 1.0, jnp.sin(phase_angle))
    parity = jnp.where(harmonic % 2 == 0, 1.0, -1.0)
    first_der = jnp.where(harmonic == 0, 0.0, 0.5 * parity * jnp.cos(phase_angle) / sine_safe)
    second = jnp.where(
        harmonic == 0,
        -(period_count * period_count + 2) / 12.0,
        -parity / (2.0 * sine_safe * sine_safe),
    )
    return OMEGA * first_der - NU_T * OMEGA * OMEGA * second


def table_lookup(table_values, instance_lag, period_count):
    harmonic = jnp.arange(period_count, dtype=jnp.int32)
    return jnp.sum(
        jnp.where(instance_lag[:, None] == harmonic[None, :], table_values[None, :], 0.0), axis=1
    )


def primitives(cells):
    density = cells[0] + cells[1]
    vel_ax = cells[2] / density
    vel_circ = cells[3] / density
    vel_rad = cells[4] / density
    fraction = cells[6]
    gamma_term = fraction / (G_LIQ - 1.0) + (1.0 - fraction) / (G_GAS - 1.0)
    stiff_term = fraction * (G_LIQ * P_LIQ / (G_LIQ - 1.0))
    kinetic = 0.5 * density * (vel_ax * vel_ax + vel_circ * vel_circ + vel_rad * vel_rad)
    pressure = (cells[5] - kinetic - stiff_term) / gamma_term
    sound_speed = jnp.sqrt(
        ((1.0 + 1.0 / gamma_term) * pressure + stiff_term / gamma_term) / density
    )
    return (density, vel_ax, vel_circ, pressure, sound_speed)


def sharpen(lower_val, centre, upper_val, offset):
    average = 0.5 * (lower_val + upper_val)
    difference = upper_val - lower_val
    steepness = 2.0 * (centre - average) / (jnp.abs(difference) + EPSA)
    return average + 0.5 * difference * jnp.tanh(BETA * (steepness + offset))


def physical(cells, fraction, circ_vel, pressure):
    return [
        cells[0] * circ_vel,
        cells[1] * circ_vel,
        cells[2] * circ_vel,
        cells[3] * circ_vel + pressure,
        cells[4] * circ_vel,
        (cells[5] + pressure) * circ_vel,
        fraction * circ_vel,
    ]


def face_flux(left_state, right_state, frac_left, frac_right):
    _, _, circ_left, press_left, sound_left = primitives(left_state)
    _, _, circ_right, press_right, sound_right = primitives(right_state)
    speed = jnp.maximum(jnp.abs(circ_left) + sound_left, jnp.abs(circ_right) + sound_right)
    flux_left = physical(left_state, frac_left, circ_left, press_left)
    flux_right = physical(right_state, frac_right, circ_right, press_right)
    jumps = [right_state[component] - left_state[component] for component in range(6)]
    jumps.append(frac_right - frac_left)
    return jnp.stack(
        [
            0.5 * (flux_left[component] + flux_right[component]) - 0.5 * speed * jumps[component]
            for component in range(7)
        ]
    )


def line_sweep(lower_coef, diagonal, upper_coef, right_side):

    def forward(carried, entries):
        ratio_prev, value_prev = carried
        below_coef, centre, above_coef, right_row = entries
        pivot_value = centre - below_coef * ratio_prev
        ratio_next = above_coef / pivot_value
        value_next = (right_row - below_coef[None] * value_prev) / pivot_value[None]
        return ((ratio_next, value_next), (ratio_next, value_next))

    start_state = (jnp.zeros_like(diagonal[0]), jnp.zeros_like(right_side[0]))
    _, (ratio_rows, value_rows) = lax.scan(
        forward, start_state, (lower_coef, diagonal, upper_coef, right_side)
    )

    def backward(following, entries):
        ratio_row, value_row = entries
        current = value_row - ratio_row[None] * following
        return (current, current)

    _, solved = lax.scan(
        backward, jnp.zeros_like(right_side[0]), (ratio_rows, value_rows), reverse=True
    )
    return solved


def local(flow_state, thinc_flags):
    own_slab = flow_state[0]
    period_count = lax.axis_size("inst")
    own_index = lax.axis_index("inst")
    table_values = spectral_table(period_count)
    instance_lag = (
        jnp.arange(lax.axis_size("inst") * 1, dtype=jnp.int32) - own_index
    ) % period_count
    weights = table_lookup(table_values, instance_lag, period_count)
    spectral = lax.psum_scatter(
        weights[:, None, None, None, None] * flow_state, "inst", scatter_dimension=0, tiled=True
    )[0]
    padded = extended(own_slab, (("circ", 2),), 2)
    circ_width = own_slab.shape[2]
    fraction = padded[6]
    flagged = (thinc_flags[0] > 0)[:, :, None]
    frac_back2 = fraction[:, 0:circ_width]
    frac_back1 = fraction[:, 1 : circ_width + 1]
    frac_here = fraction[:, 2 : circ_width + 2]
    frac_next = fraction[:, 3 : circ_width + 3]
    frac_left = jnp.where(flagged, sharpen(frac_back2, frac_back1, frac_here, 1.0), frac_back1)
    frac_right = jnp.where(flagged, sharpen(frac_back1, frac_here, frac_next, -1.0), frac_here)
    fluxes = face_flux(padded[:, :, 1 : circ_width + 1], own_slab, frac_left, frac_right)
    upper_flux = shifted(fluxes[:, :, 0:1], "circ", -1)
    residual = jnp.concatenate([fluxes[:, :, 1:], upper_flux], axis=2) - fluxes + spectral
    _, vel_ax, _, _, sound_speed = primitives(own_slab)
    radius = jnp.abs(vel_ax) + sound_speed
    coupling = -ALPHA * radius
    diagonal = DIAG0 + 2.0 * ALPHA * radius
    right_side = -residual
    field_count = own_slab.shape[0]
    ax_cells = own_slab.shape[1]
    interior = ax_cells - 1
    positions = jnp.arange(interior, dtype=jnp.int32)[:, None, None, None]
    plane_shape = (interior, 1) + radius.shape[1:]
    unit_first = jnp.broadcast_to((positions == 0).astype(jnp.float32), plane_shape)
    unit_last = jnp.broadcast_to((positions == interior - 1).astype(jnp.float32), plane_shape)
    stacked = jnp.concatenate(
        [jnp.swapaxes(right_side[:, :interior], 0, 1), unit_first, unit_last], axis=1
    )
    solved_local = line_sweep(
        coupling[:interior], diagonal[:interior], coupling[:interior], stacked
    )
    y_first = solved_local[0, :field_count]
    v_first = solved_local[0, field_count]
    w_first = solved_local[0, field_count + 1]
    y_last = solved_local[interior - 1, :field_count]
    v_last = solved_local[interior - 1, field_count]
    w_last = solved_local[interior - 1, field_count + 1]
    coup_first = coupling[0]
    coup_inner = coupling[interior - 1]
    coup_sep = coupling[ax_cells - 1]
    own_lower = -coup_sep * coup_first * v_last
    own_diag = diagonal[ax_cells - 1] - coup_sep * coup_inner * w_last
    own_rhs = right_side[:, ax_cells - 1] - coup_sep[None] * y_last
    give_first = coup_first * v_first
    give_last = coup_inner * w_first
    following = from_behind(
        jnp.concatenate([give_first[None], give_last[None], y_first], axis=0), "ax", -1
    )
    sep_rows = jnp.concatenate(
        [
            own_lower[None],
            (own_diag - coup_sep * following[0])[None],
            (-coup_sep * following[1])[None],
            own_rhs - coup_sep[None] * following[2:],
        ],
        axis=0,
    )
    gathered = lax.all_gather(sep_rows[None], "ax", axis=0, tiled=True)
    red_lower = gathered[:, 0]
    red_diag = gathered[:, 1]
    red_upper = gathered[:, 2]
    red_rhs = gathered[:, 3:]
    separators = line_sweep(red_lower, red_diag, red_upper, red_rhs)
    ax_index = lax.axis_index("ax")
    own_value = lax.dynamic_index_in_dim(separators, ax_index, 0, keepdims=False)
    prev_value = lax.dynamic_index_in_dim(
        separators, jnp.maximum(ax_index - 1, 0), 0, keepdims=False
    ) * (ax_index > 0).astype(jnp.float32)
    y_part = solved_local[:, :field_count]
    v_part = solved_local[:, field_count]
    w_part = solved_local[:, field_count + 1]
    interior_delta = (
        y_part
        - (coup_first[None] * v_part)[:, None] * prev_value[None]
        - (coup_inner[None] * w_part)[:, None] * own_value[None]
    )
    delta = jnp.swapaxes(jnp.concatenate([interior_delta, own_value[None]], axis=0), 0, 1)
    return (own_slab + delta)[None]


def solution(mesh):
    return jax.shard_map(
        local,
        mesh=mesh,
        in_specs=(P("inst", None, "ax", "circ", None), P("inst", "ax", "circ")),
        out_specs=P("inst", None, "ax", "circ", None),
        check_vma=False,
    )
```

profile of v0, /device:TPU:0, one launch (start us, length us, event | category | flops | bytes accessed | tf_op | source)
XLA Modules:
  0.0 217.6 jit_solution(2924324364586685612)
XLA Ops:
  6.8 3.9 %broadcast_multiply_fusion = f32[2,7,8,64,128]{4,3,2,1,0:T(8,128)} fusion(f32[7,8,64,128]{3,2,1,0:T(8,128)} %bitcast.432, f32[2]{0:T(128)S(1)} %fusion.75), kind=kLoop, calls=%fused_computation.32 | loop fusion | flops 917504 | bytes 5505032 | tf_op jit(solution)/shard_map/mul | solution.py:151
  12.3 3.0 %collective-permute-start = (f32[7,8,2,128]{3,2,1,0:T(2,128)S(1)}, f32[7,8,2,128]{3,2,1,0:T(2,128)S(1)}, u32[]{:S(2)}, u32[]{:S(2)}) collective-permute-start(f32[7,8,2,128]{3,2,1,0:T(2,128)S(1)} %get-tuple-element.542), channel_id=1, source_target_pairs={{0,1},{1,0},{2,3},{3,2},{4,5},{5,4},{6,7},{7,6},{8,9},{9,8},{10,11... | collective-permute-start | bytes 172040 | tf_op jit(solution)/shard_map/ppermute | solution.py:23
  15.4 2.1 collective-permute-done
  17.5 2.0 collective-permute-done.1
  25.9 36.8 %reduce-scatter.2.cloned.1.call-done = f32[1,7,8,64,128]{4,3,2,1,0:T(8,128)} async-done(((f32[2,7,8,64,128]{4,3,2,1,0:T(8,128)}), f32[1,7,8,64,128]{4,3,2,1,0:T(8,128)}) %reduce-scatter.2.cloned.1.call-update) | async-done | bytes 1835024 | tf_op jit(solution)/shard_map/reduce_scatter | solution.py:150
  62.7 3.2 %fusion.3 = f32[7,8,64,128]{3,2,1,0:T(8,128)S(1)} fusion(f32[7,8,64,128]{3,2,1,0:T(8,128)} %copy-done.1, f32[7,8,1,128]{3,2,1,0:T(1,128)S(1)} %collective-permute-done.2, f32[7,8,63,128]{3,2,1,0:T(8,128)} %slice.244, f32[1,7,8,64,128]{4,3,2,1,0:T(8,128)} %reduce-scatter.2.cloned.1.call-done), kind=kLoop, calls=%fused_computation.28 | loop fusion | flops 1835008 | bytes 7340032 | tf_op jit(solution)/shard_map/neg | solution.py:170
  70.2 17.0 %while.69 = (s32[]{:T(128)}, f32[64,128]{1,0:T(8,128)S(1)}, f32[9,64,128]{2,1,0:T(8,128)S(1)}, f32[7,64,128]{2,1,0:T(8,128)}, f32[7,9,64,128]{3,2,1,0:T(8,128)},...) while((s32[]{:T(128)}, f32[64,128]{1,0:T(8,128)S(1)}, ...), condition=%wide.region_3.4_spmd.clone, body=%wide.region_2.3_spmd.clone.sunk | while | flops 327683 | bytes 1475696 | solution.py:126
  70.8 1.8 bitcast_dynamic-update-slice_fusion.14
  73.3 1.8 bitcast_dynamic-update-slice_fusion.14
  75.7 1.8 bitcast_dynamic-update-slice_fusion.14
  78.1 1.8 bitcast_dynamic-update-slice_fusion.14
  80.5 1.8 bitcast_dynamic-update-slice_fusion.14
  83.0 1.8 bitcast_dynamic-update-slice_fusion.14
  85.4 1.8 bitcast_dynamic-update-slice_fusion.14
  88.8 18.1 %while.70 = (s32[]{:T(128)}, f32[9,64,128]{2,1,0:T(8,128)S(1)}, f32[7,9,64,128]{3,2,1,0:T(8,128)}, f32[7,9,64,128]{3,2,1,0:T(8,128)}, f32[7,64,128]{2,1,0:T(8,128)}, /*index=5*/s32[]{:T(128)}, s32[]{:T(128)}, s32[]{:T(128)}) while((s32[]{:T(128)}, f32[9,64,128]{2,1,0:T(8,128)S(1)}, f32[7,9,64,128]{3,2,1,0:T(8,128)}, ...), condition=%wide.region_5.6_spmd.clone, body=%wide.region_4.5_spmd.clone.sunk | while | flops 221188 | bytes 1278067 | solution.py:135
  89.5 1.8 bitcast_dynamic-update-slice_fusion.15
  92.1 1.8 bitcast_dynamic-update-slice_fusion.15
  94.7 1.8 bitcast_dynamic-update-slice_fusion.15
  97.3 1.8 bitcast_dynamic-update-slice_fusion.15
  99.9 1.8 bitcast_dynamic-update-slice_fusion.15
  102.5 1.8 bitcast_dynamic-update-slice_fusion.15
  105.1 1.8 bitcast_dynamic-update-slice_fusion.15
  110.0 2.2 %collective-permute-done.3 = f32[9,64,128]{2,1,0:T(8,128)S(1)} collective-permute-done((f32[9,64,128]{2,1,0:T(8,128)S(1)}, f32[9,64,128]{2,1,0:T(8,128)S(1)}, u32[]{:S(2)}, u32[]{:S(2)}) %collective-permute-start.3) | collective-permute-done | bytes 294944 | tf_op jit(solution)/shard_map/ppermute | solution.py:40
  116.0 36.1 %all-gather.3.cloned.1.call-done = f32[80,64,128]{2,1,0:T(8,128)} async-done(((f32[10,64,128]{2,1,0:T(8,128)}), f32[80,64,128]{2,1,0:T(8,128)}) %all-gather.3.cloned.1.call-update) | async-done | bytes 2621456 | tf_op jit(solution)/shard_map/all_gather | solution.py:210
  152.0 2.9 %slice.259 = f32[8,7,64,128]{3,2,1,0:T(8,128)} slice(f32[8,10,64,128]{3,2,1,0:T(8,128)} %bitcast.436), slice={[0:8], [3:10], [0:64], [0:128]} | slice | bytes 3670016 | tf_op jit(solution)/shard_map/slice | solution.py:214
  155.0 1.9 slice_bitcast_fusion.1
  158.3 24.7 %while.71 = (s32[]{:T(128)}, f32[64,128]{1,0:T(8,128)S(1)}, f32[7,64,128]{2,1,0:T(8,128)S(1)}, f32[8,64,128]{2,1,0:T(8,128)}, f32[8,7,64,128]{3,2,1,0:T(8,128)},...) while((s32[]{:T(128)}, f32[64,128]{1,0:T(8,128)S(1)}, ...), condition=%wide.region_7.8_spmd.clone, body=%wide.region_6.7_spmd.clone.sunk | while | flops 262147 | bytes 1246328 | solution.py:126
  184.5 20.1 %while.72 = (s32[]{:T(128)}, f32[7,64,128]{2,1,0:T(8,128)S(1)}, f32[8,7,64,128]{3,2,1,0:T(8,128)}, f32[8,7,64,128]{3,2,1,0:T(8,128)}, f32[8,64,128]{2,1,0:T(8,128)}, /*index=5*/s32[]{:T(128)}, s32[]{:T(128)}, s32[]{:T(128)}) while((s32[]{:T(128)}, f32[7,64,128]{2,1,0:T(8,128)S(1)}, f32[8,7,64,128]{3,2,1,0:T(8,128)}, ...), condition=%wide.region_9.10_spmd.clone, body=%wide.region_8.9_spmd.clone.sunk | while | flops 172036 | bytes 1015923 | solution.py:135
  187.8 1.7 bitcast_dynamic-update-slice_fusion.18
  190.3 1.7 bitcast_dynamic-update-slice_fusion.18
  192.8 1.7 bitcast_dynamic-update-slice_fusion.18
  195.3 1.7 bitcast_dynamic-update-slice_fusion.18
  (106 shorter events, 77.5 us)
Async XLA Ops:
  6.5 56.2 %reduce-scatter.2.cloned.1.call-start = ((), (), s32[]{:S(2)}) async-start(), calls=%async_computation.1 | async-start | bytes 5505024 | tf_op jit(solution)/shard_map/reduce_scatter | solution.py:150
  10.7 1.5 copy-start
  10.7 4.6 %copy-start.3 = (s32[1,8,64]{2,1,0:T(8,128)S(1)}, s32[1,8,64]{2,1,0:T(8,128)}, u32[]{:S(2)}) copy-start(s32[1,8,64]{2,1,0:T(8,128)} %param.11) | copy-start | bytes 6148
  10.8 141.3 %all-gather.3.cloned.1.call-start = ((), (), s32[]{:S(2)}) async-start(), calls=%async_computation.2 | async-start | bytes 2949120 | tf_op jit(solution)/shard_map/all_gather | solution.py:210
  12.3 5.2 %collective-permute-start = (f32[7,8,2,128]{3,2,1,0:T(2,128)S(1)}, f32[7,8,2,128]{3,2,1,0:T(2,128)S(1)}, u32[]{:S(2)}, u32[]{:S(2)}) collective-permute-start(f32[7,8,2,128]{3,2,1,0:T(2,128)S(1)} %get-tuple-element.542), channel_id=1, source_target_pairs={{0,1},{1,0},{2,3},{3,2},{4,5},{5,4},{6,7},{7,6},{8,9},{9,8},{10,11... | collective-permute-start | bytes 172040 | tf_op jit(solution)/shard_map/ppermute | solution.py:23
  15.3 4.2 %collective-permute-start.1 = (f32[7,8,2,128]{3,2,1,0:T(2,128)S(1)}, f32[7,8,2,128]{3,2,1,0:T(2,128)S(1)}, u32[]{:S(2)}, u32[]{:S(2)}) collective-permute-start(f32[7,8,2,128]{3,2,1,0:T(2,128)S(1)} %get-tuple-element.541), channel_id=1, source_target_pairs={{1,0},{0,1},{3,2},{2,3},{5,4},{4,5},{7,6},{6,7},{9,8},{8,9},{11,10... | collective-permute-start | bytes 172040 | tf_op jit(solution)/shard_map/ppermute | solution.py:26
  22.0 2.4 %copy-start.1 = (f32[7,8,64,128]{3,2,1,0:T(8,128)}, f32[7,8,64,128]{3,2,1,0:T(8,128)S(1)}, u32[]{:S(2)}) copy-start(f32[7,8,64,128]{3,2,1,0:T(8,128)S(1)} %get-tuple-element.516) | copy-start | bytes 5505028
  22.0 3.9 %collective-permute-start.2 = (f32[7,8,1,128]{3,2,1,0:T(1,128)S(1)}, f32[7,8,1,128]{3,2,1,0:T(1,128)S(1)}, u32[]{:S(2)}, u32[]{:S(2)}) collective-permute-start(f32[7,8,1,128]{3,2,1,0:T(1,128)S(1)} %slice.245), channel_id=1, source_target_pairs={{1,0},{0,1},{3,2},{2,3},{5,4},{4,5},{7,6},{6,7},{9,8},{8,9},{11,10... | collective-permute-start | bytes 86024 | tf_op jit(solution)/shard_map/ppermute | solution.py:34
  66.0 1.2 copy-start.2
  108.7 3.5 %collective-permute-start.3 = (f32[9,64,128]{2,1,0:T(8,128)S(1)}, f32[9,64,128]{2,1,0:T(8,128)S(1)}, u32[]{:S(2)}, u32[]{:S(2)}) collective-permute-start(f32[9,64,128]{2,1,0:T(8,128)S(1)} %pad_maximum_fusion.4), channel_id=1, source_target_pairs={{2,0},{4,2},{6,4},{8,6},{10,8},{12,10},{14,12},{3,1},{5,3},{7,5},{... | collective-permute-start | bytes 884744 | tf_op jit(solution)/shard_map/ppermute | solution.py:40
Sparse Core Ops, SparseCore 0:
  10.9 51.7 reduce-scatter.1
  115.0 37.0 all-gather.2
where the time goes:
time: 221 us; the launch traced here: 218 us
  other arithmetic  88.7 us (40%)
  waiting for transfers between devices  80.6 us (36%)
  local copies, waits for them, and re-layouts  29.4 us (13%)
  between operations  13.6 us (6%)
  starting transfers between devices  5.19 us (2%)
    dynamic_update_slice x45, other arithmetic, line_sweep(): lax.scan(forward, start_state, (lower_coef, diagonal, upper_coef, right_s...  68.4 us
    reduce_scatter x1, waiting for transfers between devices, local(): lax.psum_scatter(weights[:, None, None, None, None] * flow_state, 'inst',...  36.8 us
    all_gather x1, waiting for transfers between devices, local(): gathered = lax.all_gather(sep_rows[None], 'ax', axis=0, tiled=True)  36.1 us
    mul x15, local copies, waits for them, and re-layouts, backward(): current = value_row - ratio_row[None] * following  11.4 us
    another operation x4, local copies, waits for them, and re-layouts  6.07 us
  transfers between devices with their start and end apart: 6, of which 6 were waited for; matrix products, arithmetic and copies ran while one was open for 2% of the time, Pallas kernels for 0%

commit v1 on v0

v1 whole, which is shorter than its diff:
```python
import functools
import math

import jax
import jax.numpy as jnp
import numpy as np
from jax import lax
from jax.experimental import pallas as pl
from jax.experimental.pallas import tpu as pltpu
from jax.sharding import PartitionSpec as P

G_LIQ = 4.4
P_LIQ = 6.0
G_GAS = 1.4
BETA = 1.6
EPSA = 0.1
ALPHA = 4.0
DIAG0 = 0.016
OMEGA = 1.0
NU_T = 0.25
MESH = pl.DeviceIdType.MESH
TILE = 8


def spectral_weights(count):
    weights = []
    for k in range(count):
        if k == 0:
            first, second = 0.0, -(count * count + 2) / 12.0
        else:
            angle = math.pi * k / count
            parity = 1.0 if k % 2 == 0 else -1.0
            first = 0.5 * parity * math.cos(angle) / math.sin(angle)
            second = -parity / (2.0 * math.sin(angle) ** 2)
        weights.append(float(np.float32(OMEGA * first - NU_T * OMEGA * OMEGA * second)))
    return weights


def sharpen(lower_val, centre, upper_val, offset):
    average = 0.5 * (lower_val + upper_val)
    difference = upper_val - lower_val
    steepness = 2.0 * (centre - average) / (jnp.abs(difference) + EPSA)
    return average + 0.5 * difference * jnp.tanh(BETA * (steepness + offset))


def primitives(q):
    density = q[0] + q[1]
    inv = 1.0 / density
    vel_ax = q[2] * inv
    vel_circ = q[3] * inv
    vel_rad = q[4] * inv
    fraction = q[6]
    gamma_term = fraction / (G_LIQ - 1.0) + (1.0 - fraction) / (G_GAS - 1.0)
    stiff_term = fraction * (G_LIQ * P_LIQ / (G_LIQ - 1.0))
    kinetic = 0.5 * (vel_ax * q[2] + vel_circ * q[3] + vel_rad * q[4])
    inv_gamma = 1.0 / gamma_term
    pressure = (q[5] - kinetic - stiff_term) * inv_gamma
    sound = jnp.sqrt((pressure + (pressure + stiff_term) * inv_gamma) * inv)
    return vel_ax, vel_circ, pressure, sound


def kernel(sizes, weights, q_hbm, flag_ref, out_hbm, pad, prim, flux, bg, iv, piv, phi, psi, rem,
           halo_out, halo_in, chain_out, chain_in, coef, ps, zrecv, ag_out, ag_in,
           load_sem, ysend, yrecv, hsend, hrecv, csend, crecv, zsend, zrecv_sem, fsend, frecv, osem):
    n_inst, n_ax, n_circ, rows, width, radial = sizes
    fields = 7
    chunks = width // TILE
    block = 4 if rows % 4 == 0 else 1
    i, me, c = lax.axis_index("inst"), lax.axis_index("ax"), lax.axis_index("circ")
    core = lax.rem(me, 2)
    base = me - core
    sibling = base + 1 - core
    above, below = lax.rem(c + 1, n_circ), lax.rem(c + n_circ - 1, n_circ)

    def tile(j):
        return pl.ds(pl.multiple_of(j * TILE, TILE), TILE)

    load = pltpu.make_async_copy(q_hbm.at[0], pad.at[:, :, pl.ds(TILE, width), :], load_sem)
    load.start()

    barrier = pltpu.get_barrier_semaphore()
    for k in range(1, n_inst):
        pl.semaphore_signal(barrier, inc=1, device_id=(lax.rem(i + k, n_inst), me, c), device_id_type=MESH)
    for k in range(1, n_ax):
        pl.semaphore_signal(barrier, inc=1, device_id=(i, lax.rem(me + k, n_ax), c), device_id_type=MESH)
    for other in (above, below):
        pl.semaphore_signal(barrier, inc=1, device_id=(i, me, other), device_id_type=MESH)
    pl.semaphore_wait(barrier, n_inst + n_ax)

    def ycopy(k, j):
        return pltpu.make_async_remote_copy(
            src_ref=q_hbm.at[0, :, :, tile(j), :], dst_ref=rem.at[k - 1, :, :, tile(j), :],
            send_sem=ysend.at[k - 1, j], recv_sem=yrecv.at[k - 1, j],
            device_id=(lax.rem(i + k, n_inst), me, c), device_id_type=MESH)

    for j in range(chunks):
        for k in range(1, n_inst):
            ycopy(k, j).start()

    load.wait()

    for f in range(fields):
        halo_out[0, f] = pad[f, :, TILE + width - 1, :]
        halo_out[1, f] = pad[f, :, TILE, :]
    halo_out[0, fields] = pad[fields - 1, :, TILE + width - 2, :]
    halo_out[1, fields] = pad[fields - 1, :, TILE + 1, :]
    halo_out[0, fields + 1] = flag_ref[:, 0, :]
    halo_out[1, fields + 1] = flag_ref[:, 0, :]
    halos = [
        pltpu.make_async_remote_copy(
            src_ref=halo_out.at[side], dst_ref=halo_in.at[side], send_sem=hsend.at[side],
            recv_sem=hrecv.at[side], device_id=(i, me, (above, below)[side]), device_id_type=MESH)
        for side in range(2)
    ]
    for copy in halos:
        copy.start()

    def own_tile(j, carry):
        at = tile(j + 1)
        here = tile(j)
        for a0 in range(0, rows, block):
            part = pl.ds(a0, block)
            vel_ax, vel_circ, pressure, sound = primitives([pad[f, part, at, :] for f in range(fields)])
            prim[0, part, at, :] = vel_circ
            prim[1, part, at, :] = pressure
            prim[2, part, at, :] = jnp.abs(vel_circ) + sound
            iv[part, here, :] = (1.0 / ALPHA) / (jnp.abs(vel_ax) + sound)
        pivots, firsts = [], []
        for a in range(rows):
            value = 2.0 + DIAG0 * iv[a, here, :]
            if a:
                value = value - pivots[-1]
            pivots.append(1.0 / value)
            firsts.append(pivots[-1] * firsts[-1] if a else pivots[-1])
        low, high = firsts[-1], pivots[-1]
        for a in reversed(range(rows)):
            if a < rows - 1:
                low = firsts[a] + pivots[a] * low
                high = pivots[a] * high
            piv[a, here, :] = pivots[a]
            phi[a, here, :] = low
            psi[a, here, :] = high
        return carry

    lax.fori_loop(0, chunks, own_tile, 0)

    last = rows - 1

    def chain_copy(side, target):
        return pltpu.make_async_remote_copy(
            src_ref=chain_out.at[side], dst_ref=chain_in.at[side], send_sem=csend.at[side],
            recv_sem=crecv.at[side], device_id=(i, target, c), device_id_type=MESH)

    up_copy = chain_copy(0, jnp.minimum(me + 1, n_ax - 1))
    down_copy = chain_copy(1, jnp.maximum(me - 1, 0))

    def chain_up():
        @pl.when(me == 0)
        def _():
            chain_in[0, 0] = jnp.zeros((width, radial), jnp.float32)
            chain_in[0, 1] = jnp.ones((width, radial), jnp.float32)

        @pl.when(me > 0)
        def _():
            up_copy.wait_recv()

        wall, scale = chain_in[0, 0], chain_in[0, 1]
        den = 1.0 / (1.0 - wall * phi[0])
        mix = phi[last] * wall * den
        following = scale * phi[last] * den
        chain_out[0, 0] = psi[last] + mix * psi[0]
        chain_out[0, 1] = following

        @pl.when(me < n_ax - 1)
        def _():
            up_copy.start()

        inverse = 1.0 / following
        coef[0] = inverse
        coef[1] = mix * inverse

    def chain_down():
        @pl.when(me == n_ax - 1)
        def _():
            chain_in[1, 0] = jnp.zeros((width, radial), jnp.float32)
            chain_in[1, 1] = jnp.ones((width, radial), jnp.float32)

        @pl.when(me < n_ax - 1)
        def _():
            down_copy.wait_recv()

        wall, scale = chain_in[1, 0], chain_in[1, 1]
        den = 1.0 / (1.0 - wall * psi[last])
        mix = psi[0] * wall * den
        following = scale * psi[0] * den
        chain_out[1, 0] = phi[0] + mix * phi[last]
        chain_out[1, 1] = following

        @pl.when(me > 0)
        def _():
            down_copy.start()

        inverse = 1.0 / following
        coef[2] = inverse
        coef[3] = mix * inverse

    lower_half = me < n_ax // 2
    pl.when(lower_half)(chain_up)
    pl.when(jnp.logical_not(lower_half))(chain_down)

    for copy in halos:
        copy.wait_recv()
    sub = lax.broadcasted_iota(jnp.int32, (TILE, radial), 0)
    top = chunks + 1
    for a in range(rows):
        for side, t, edge in ((0, 0, TILE - 1), (1, top, 0)):
            cells = []
            for f in range(fields):
                near = jnp.broadcast_to(halo_in[side, f, pl.ds(a, 1), :], (TILE, radial))
                if f == fields - 1:
                    far = jnp.broadcast_to(halo_in[side, fields, pl.ds(a, 1), :], (TILE, radial))
                    near = jnp.where(sub == edge, near, far)
                cells.append(near)
                pad[f, a, pl.ds(t * TILE, TILE), :] = near
            _, vel_circ, pressure, sound = primitives(cells)
            prim[0, a, pl.ds(t * TILE, TILE), :] = vel_circ
            prim[1, a, pl.ds(t * TILE, TILE), :] = pressure
            prim[2, a, pl.ds(t * TILE, TILE), :] = jnp.abs(vel_circ) + sound

    def behind(low, mid, by):
        return jnp.where(sub < by, pltpu.roll(low, by, 0), pltpu.roll(mid, by, 0))

    def ahead(mid, high):
        return jnp.where(sub == TILE - 1, pltpu.roll(high, TILE - 1, 0), pltpu.roll(mid, TILE - 1, 0))

    def face_tile(j, a, flagged):
        low, mid, high = tile(j), tile(j + 1), tile(jnp.minimum(j + 2, top))
        frac_low, frac_here, frac_high = (pad[fields - 1, a, t, :] for t in (low, mid, high))
        back1 = behind(frac_low, frac_here, 1)
        back2 = behind(frac_low, frac_here, 2)
        following = ahead(frac_here, frac_high)
        frac_left = jnp.where(flagged, sharpen(back2, back1, frac_here, 1.0), back1)
        frac_right = jnp.where(flagged, sharpen(back1, frac_here, following, -1.0), frac_here)
        vel_r, press_r, fast_r = (prim[s, a, mid, :] for s in range(3))
        vel_l, press_l, fast_l = (behind(prim[s, a, low, :], prim[s, a, mid, :], 1) for s in range(3))
        half = 0.5 * jnp.maximum(fast_l, fast_r)
        take_l, take_r = 0.5 * vel_l + half, 0.5 * vel_r - half
        for f in range(fields):
            if f < fields - 1:
                right = pad[f, a, mid, :]
                left = behind(pad[f, a, low, :], right, 1)
            else:
                left, right = frac_left, frac_right
            value = left * take_l + right * take_r
            if f == 3:
                value = value + 0.5 * (press_l + press_r)
            if f == 5:
                value = value + 0.5 * (press_l * vel_l + press_r * vel_r)
            flux[f, a, low, :] = value

    def faces(j, carry):
        for a in range(rows):
            face_tile(j, a, flag_ref[a, tile(j), :] > 0.5)
        return carry

    lax.fori_loop(0, chunks, faces, 0)
    for a in range(rows):
        face_tile(chunks, a, jnp.broadcast_to(halo_in[1, fields + 1, pl.ds(a, 1), :], (TILE, radial)) > 0.5)

    def right_side(j, carry):
        for a in range(rows):
            scale = iv[a, tile(j), :]
            for f in range(fields):
                here = flux[f, a, tile(j), :]
                change = ahead(here, flux[f, a, tile(j + 1), :]) - here
                bg[f, a, tile(j), :] = -scale * (change + weights[0] * pad[f, a, tile(j + 1), :])
        return carry

    lax.fori_loop(0, chunks, right_side, 0)

    pl.when(lower_half)(chain_down)
    pl.when(jnp.logical_not(lower_half))(chain_up)

    wall_l, wall_u = chain_in[0, 0], chain_in[1, 0]
    keep_l, keep_u = 1.0 - wall_l * phi[0], 1.0 - wall_u * psi[last]
    cross_l, cross_u = wall_l * phi[last], wall_u * psi[0]
    inv_det = 1.0 / (keep_l * keep_u - cross_l * cross_u)
    coef[4] = wall_l * keep_u * inv_det
    coef[5] = wall_l * cross_u * inv_det
    coef[6] = wall_u * cross_l * inv_det
    coef[7] = wall_u * keep_l * inv_det

    def span(ref, *index):
        return ref.at[index]

    def zcopy(j, step):
        dest = lax.rem(base + lax.rem(j, 2) + 2 * step, n_ax)
        slot = lax.rem(me - dest + n_ax, n_ax)
        pick = jnp.where(me < dest, 0, 1)
        return pltpu.make_async_remote_copy(
            src_ref=ps.at[pick, :, tile(j), :], dst_ref=zrecv.at[slot, :, tile(j), :],
            send_sem=zsend.at[j], recv_sem=zrecv_sem.at[j],
            device_id=(i, dest, c), device_id_type=MESH)

    def forward_copy(j):
        return pltpu.make_async_remote_copy(
            src_ref=ag_out.at[:, :, tile(j), :], dst_ref=ag_in.at[:, :, tile(j), :],
            send_sem=fsend.at[j], recv_sem=frecv.at[j],
            device_id=(i, sibling, c), device_id_type=MESH)

    def out_copy(j):
        return pltpu.make_async_copy(bg.at[:, :, tile(j), :], out_hbm.at[0, :, :, tile(j), :], osem.at[j])

    def reduce_chunk(j):
        at = tile(j)
        for k in range(1, n_inst):
            ycopy(k, j).wait_recv()

        def one_field(f, carry):
            running = None
            values = []
            for a in range(rows):
                other = weights[1] * rem[0, f, a, at, :]
                for k in range(2, n_inst):
                    other = other + weights[k] * rem[k - 1, f, a, at, :]
                value = bg[f, a, at, :] - iv[a, at, :] * other
                running = piv[a, at, :] * (value if a == 0 else value + running)
                values.append(running)
            solved = values[-1]
            bg[f, last, at, :] = solved
            for a in reversed(range(last)):
                solved = values[a] + piv[a, at, :] * solved
                bg[f, a, at, :] = solved
            ps[0, f, at, :] = coef[0, at, :] * values[-1] + coef[1, at, :] * solved
            ps[1, f, at, :] = coef[2, at, :] * solved + coef[3, at, :] * values[-1]
            return carry

        lax.fori_loop(0, fields, one_field, 0)

        @pl.when(core != lax.rem(j, 2))
        def _():
            zcopy(j, 0).start()

        for step in range(1, n_ax // 2):
            zcopy(j, step).start()

    def gather_chunk(j):
        at = tile(j)

        @pl.when(core == lax.rem(j, 2))
        def _():
            landed = zrecv.at[pl.ds(1, n_ax - 1), :, at, :]
            pltpu.make_async_copy(landed, landed, zrecv_sem.at[j]).wait()

            def one_field(f, carry):
                down = jnp.zeros((TILE, radial), jnp.float32)
                up = jnp.zeros((TILE, radial), jnp.float32)
                for slot in range(1, n_ax):
                    source = lax.rem(me + slot, n_ax)
                    value = zrecv[slot, f, at, :]
                    down = down + jnp.where(source < base, value, 0.0)
                    up = up + jnp.where(source > base + 1, value, 0.0)
                beside = jnp.where(core == 0, zrecv[1, f, at, :], zrecv[n_ax - 1, f, at, :])
                ag_out[0, f, at, :] = down + jnp.where(core == 0, ps[0, f, at, :], 0.0)
                ag_out[1, f, at, :] = up + jnp.where(core == 0, 0.0, ps[1, f, at, :])
                ag_in[0, f, at, :] = down + jnp.where(core == 0, 0.0, beside)
                ag_in[1, f, at, :] = up + jnp.where(core == 0, beside, 0.0)
                return carry

            lax.fori_loop(0, fields, one_field, 0)
            forward_copy(j).start()

    def finish_chunk(j):
        at = tile(j)

        @pl.when(core != lax.rem(j, 2))
        def _():
            forward_copy(j).wait_recv()

        def one_field(f, carry):
            low = chain_in[0, 1, at, :] * ag_in[0, f, at, :]
            high = chain_in[1, 1, at, :] * ag_in[1, f, at, :]
            first = bg[f, 0, at, :] + low * phi[0, at, :] + high * psi[0, at, :]
            final = bg[f, last, at, :] + low * phi[last, at, :] + high * psi[last, at, :]
            low = low + coef[4, at, :] * first + coef[5, at, :] * final
            high = high + coef[6, at, :] * first + coef[7, at, :] * final
            for a in range(rows):
                delta = bg[f, a, at, :] + low * phi[a, at, :] + high * psi[a, at, :]
                bg[f, a, at, :] = pad[f, a, tile(j + 1), :] + delta
            return carry

        lax.fori_loop(0, fields, one_field, 0)
        out_copy(j).start()

    def step(j, carry):
        @pl.when(j < chunks)
        def _():
            reduce_chunk(j)

        @pl.when(jnp.logical_and(j >= 1, j <= chunks))
        def _():
            gather_chunk(j - 1)

        @pl.when(j >= 2)
        def _():
            finish_chunk(j - 2)

        return carry

    lax.fori_loop(0, chunks + 2, step, 0)

    for copy in halos:
        copy.wait_send()

    @pl.when(me < n_ax - 1)
    def _():
        up_copy.wait_send()

    @pl.when(me > 0)
    def _():
        down_copy.wait_send()

    def drain(j, carry):
        for k in range(1, n_inst):
            ycopy(k, j).wait_send()

        @pl.when(core != lax.rem(j, 2))
        def _():
            zcopy(j, 0).wait_send()

        for s in range(1, n_ax // 2):
            zcopy(j, s).wait_send()

        @pl.when(core == lax.rem(j, 2))
        def _():
            forward_copy(j).wait_send()

        out_copy(j).wait()
        return carry

    lax.fori_loop(0, chunks, drain, 0)


def local(mesh_shape, flow_state, thinc_flags):
    n_inst, n_ax, n_circ = mesh_shape["inst"], mesh_shape["ax"], mesh_shape["circ"]
    _, fields, rows, width, radial = flow_state.shape
    chunks = width // TILE
    flags = jnp.broadcast_to(thinc_flags[0].astype(jnp.float32)[:, :, None], (rows, width, radial))
    f32 = jnp.float32
    scratch = [
        pltpu.VMEM((fields, rows, width + 2 * TILE, radial), f32),
        pltpu.VMEM((3, rows, width + 2 * TILE, radial), f32),
        pltpu.VMEM((fields, rows, width + TILE, radial), f32),
        pltpu.VMEM((fields, rows, width, radial), f32),
        pltpu.VMEM((rows, width, radial), f32),
        pltpu.VMEM((rows, width, radial), f32),
        pltpu.VMEM((rows, width, radial), f32),
        pltpu.VMEM((rows, width, radial), f32),
        pltpu.VMEM((n_inst - 1, fields, rows, width, radial), f32),
        pltpu.VMEM((2, fields + 2, rows, radial), f32),
        pltpu.VMEM((2, fields + 2, rows, radial), f32),
        pltpu.VMEM((2, 2, width, radial), f32),
        pltpu.VMEM((2, 2, width, radial), f32),
        pltpu.VMEM((8, width, radial), f32),
        pltpu.VMEM((2, fields, width, radial), f32),
        pltpu.VMEM((n_ax, fields, width, radial), f32),
        pltpu.VMEM((2, fields, width, radial), f32),
        pltpu.VMEM((2, fields, width, radial), f32),
        pltpu.SemaphoreType.DMA,
        pltpu.SemaphoreType.DMA((n_inst - 1, chunks)),
        pltpu.SemaphoreType.DMA((n_inst - 1, chunks)),
        pltpu.SemaphoreType.DMA((2,)),
        pltpu.SemaphoreType.DMA((2,)),
        pltpu.SemaphoreType.DMA((2,)),
        pltpu.SemaphoreType.DMA((2,)),
        pltpu.SemaphoreType.DMA((chunks,)),
        pltpu.SemaphoreType.DMA((chunks,)),
        pltpu.SemaphoreType.DMA((chunks,)),
        pltpu.SemaphoreType.DMA((chunks,)),
        pltpu.SemaphoreType.DMA((chunks,)),
    ]
    return pl.pallas_call(
        functools.partial(
            kernel, (n_inst, n_ax, n_circ, rows, width, radial), spectral_weights(n_inst)
        ),
        out_shape=jax.ShapeDtypeStruct(flow_state.shape, f32),
        in_specs=[pl.BlockSpec(memory_space=pl.ANY), pl.BlockSpec(memory_space=pltpu.VMEM)],
        out_specs=pl.BlockSpec(memory_space=pl.ANY),
        scratch_shapes=scratch,
        compiler_params=pltpu.CompilerParams(
            collective_id=0, has_side_effects=True, vmem_limit_bytes=48 * 1024 * 1024
        ),
    )(flow_state, flags)


def solution(mesh):
    return jax.shard_map(
        functools.partial(local, dict(mesh.shape)),
        mesh=mesh,
        in_specs=(P("inst", None, "ax", "circ", None), P("inst", "ax", "circ")),
        out_specs=P("inst", None, "ax", "circ", None),
        check_vma=False,
    )
```

time: 221 us -> 55.7 us (0.25); the launches traced: 218 us -> 55.6 us
  other arithmetic: 88.7 us -> 0.69 us
  waiting for transfers between devices: 80.6 us -> 0 us
  Pallas kernels: 0 us -> 52 us
  local copies, waits for them, and re-layouts: 29.4 us -> 2.85 us
  between operations: 13.6 us -> 0.03 us
  starting transfers between devices: 5.19 us -> 0 us
    dynamic_update_slice x45 -> x0, other arithmetic: 68.4 us -> none  [line_sweep(): lax.scan(forward, start_state, (lower_coef, diagonal, upper_coef, right_s...]
    pallas_call x0 -> x1, Pallas kernels: none -> 52 us  [local(): pl.pallas_call(functools.partial(kernel, (n_inst, n_ax, n_circ, rows, wid...]
    reduce_scatter x1 -> x0, waiting for transfers between devices: 36.8 us -> none  [local(): lax.psum_scatter(weights[:, None, None, None, None] * flow_state, 'inst',...]
    all_gather x1 -> x0, waiting for transfers between devices: 36.1 us -> none  [local(): gathered = lax.all_gather(sep_rows[None], 'ax', axis=0, tiled=True)]
    mul x16 -> x0, local copies, waits for them, and re-layouts: 12.4 us -> none  [the longest x15 11.4 us: backward(): current = value_row - ratio_row[None] * following]
    ppermute x4 -> x0, waiting for transfers between devices: 7.79 us -> none  [the longest x1 2.18 us: from_behind(): return lax.ppermute(value, axis, pairs)]
    mul x4 -> x0, other arithmetic: 6.79 us -> none  [the longest x1 3.93 us: local(): weights[:, None, None, None, None] * flow_state]
    another operation x4 -> x0, local copies, waits for them, and re-layouts: 6.07 us -> none
  transfers between devices with their start and end apart: 6 -> 0, of which waited for: 6 -> 0; matrix products, arithmetic and copies ran while one was open for 2% -> 0% of each run, Pallas kernels for 0% -> 0%
where the time goes in v1:
time: 55.7 us; the launch traced here: 55.6 us
  Pallas kernels  52 us (93%)
  local copies, waits for them, and re-layouts  2.85 us (5%)
  other arithmetic  0.69 us (1%)
    pallas_call x1, Pallas kernels, local(): pl.pallas_call(functools.partial(kernel, (n_inst, n_ax, n_circ, rows, wid...  52 us
    unnamed x3, local copies, waits for them, and re-layouts  2.73 us

profile of v1, /device:TPU:0, one launch (start us, length us, event | category | flops | bytes accessed | tf_op | source)
XLA Modules:
  0.0 55.6 jit_solution(18345131923685500376)
XLA Ops:
  0.0 0.7 %convert_bitcast_fusion = f32[8,64]{1,0:T(8,128)S(1)} fusion(s32[1,8,64]{2,1,0:T(8,128)} %param.3), kind=kLoop, calls=%fused_computation | loop fusion | flops 512 | bytes 4096 | tf_op jit(solution)/shard_map/convert_element_type | solution.py:448
  0.7 0.1 broadcast_in_dim.2.flag_ref
  0.8 0.0 copy-start
  0.8 1.5 %copy-done = f32[1,7,8,64,128]{4,3,2,1,0:T(8,128)S(1)} copy-done((f32[1,7,8,64,128]{4,3,2,1,0:T(8,128)S(1)}, f32[1,7,8,64,128]{4,3,2,1,0:T(8,128)}, u32[]{:S(2)}) %copy-start) | copy-done | bytes 1835032
  2.3 52.0 %shard_map.28 = f32[1,7,8,64,128]{4,3,2,1,0:T(8,128)S(1)} custom-call(f32[1,7,8,64,128]{4,3,2,1,0:T(8,128)S(1)} %copy-done, f32[8,64,128]{2,1,0:T(8,128)S(1)} %broadcast_in_dim.2.flag_ref), custom_call_target="tpu_custom_call" | custom-call | tf_op jit(solution)/shard_map/pallas_call | solution.py:482
  54.3 1.2 %copy.4 = f32[1,7,8,64,128]{4,3,2,1,0:T(8,128)} copy(f32[1,7,8,64,128]{4,3,2,1,0:T(8,128)S(1)} %shard_map.28) | data formatting | bytes 3670016
Async XLA Ops:
  0.8 1.5 %copy-start = (f32[1,7,8,64,128]{4,3,2,1,0:T(8,128)S(1)}, f32[1,7,8,64,128]{4,3,2,1,0:T(8,128)}, u32[]{:S(2)}) copy-start(f32[1,7,8,64,128]{4,3,2,1,0:T(8,128)} %q_hbm.1) | copy-start | bytes 5505028

commit v2 on v1

--- a/solution.py
+++ b/solution.py
@@ -20,6 +20,7 @@
 NU_T = 0.25
 MESH = pl.DeviceIdType.MESH
 TILE = 8
+PIECES = ((0, 4), (4, 2), (6, 1))
 
 
 def spectral_weights(count):
@@ -59,7 +60,7 @@
     return vel_ax, vel_circ, pressure, sound
 
 
-def kernel(sizes, weights, q_hbm, flag_ref, out_hbm, pad, prim, flux, bg, iv, piv, phi, psi, rem,
+def kernel(sizes, weights, q_hbm, flag_ref, out_hbm, pad, prim, flux, bg, iv, piv, phi, psi, rem, flag_wide,
            halo_out, halo_in, chain_out, chain_in, coef, ps, zrecv, ag_out, ag_in,
            load_sem, ysend, yrecv, hsend, hrecv, csend, crecv, zsend, zrecv_sem, fsend, frecv, osem):
     n_inst, n_ax, n_circ, rows, width, radial = sizes
@@ -87,15 +88,26 @@
         pl.semaphore_signal(barrier, inc=1, device_id=(i, me, other), device_id_type=MESH)
     pl.semaphore_wait(barrier, n_inst + n_ax)
 
-    def ycopy(k, j):
+    units = [(j, 0, fields) for j in range(chunks - 1)]
+    units += [(chunks - 1, f0, nf) for f0, nf in PIECES]
+
+    def ycopy(k, u, j, f0, nf):
         return pltpu.make_async_remote_copy(
-            src_ref=q_hbm.at[0, :, :, tile(j), :], dst_ref=rem.at[k - 1, :, :, tile(j), :],
-            send_sem=ysend.at[k - 1, j], recv_sem=yrecv.at[k - 1, j],
+            src_ref=q_hbm.at[0, pl.ds(f0, nf), :, tile(j), :],
+            dst_ref=rem.at[k - 1, pl.ds(f0, nf), :, tile(j), :],
+            send_sem=ysend.at[k - 1, u], recv_sem=yrecv.at[k - 1, u],
             device_id=(lax.rem(i + k, n_inst), me, c), device_id_type=MESH)
 
-    for j in range(chunks):
+    for u, (j, f0, nf) in enumerate(units):
         for k in range(1, n_inst):
-            ycopy(k, j).start()
+            ycopy(k, u, j, f0, nf).start()
+
+    flags = flag_ref[0].astype(jnp.float32)
+    line = lax.broadcasted_iota(jnp.int32, flags.shape, 0)
+    for a in range(rows):
+        flag_wide[a] = lax.dot_general(
+            jnp.where(line == a, flags, 0.0), jnp.ones((rows, radial), jnp.float32),
+            (((0,), (0,)), ((), ())), preferred_element_type=jnp.float32)
 
     load.wait()
 
@@ -104,8 +116,9 @@
         halo_out[1, f] = pad[f, :, TILE, :]
     halo_out[0, fields] = pad[fields - 1, :, TILE + width - 2, :]
     halo_out[1, fields] = pad[fields - 1, :, TILE + 1, :]
-    halo_out[0, fields + 1] = flag_ref[:, 0, :]
-    halo_out[1, fields + 1] = flag_ref[:, 0, :]
+    first_flags = jnp.broadcast_to(flags[:, 0:1], (rows, radial))
+    halo_out[0, fields + 1] = first_flags
+    halo_out[1, fields + 1] = first_flags
     halos = [
         pltpu.make_async_remote_copy(
             src_ref=halo_out.at[side], dst_ref=halo_in.at[side], send_sem=hsend.at[side],
@@ -260,7 +273,7 @@
 
     def faces(j, carry):
         for a in range(rows):
-            face_tile(j, a, flag_ref[a, tile(j), :] > 0.5)
+            face_tile(j, a, flag_wide[a, tile(j), :] > 0.5)
         return carry
 
     lax.fori_loop(0, chunks, faces, 0)
@@ -290,17 +303,28 @@
     coef[6] = wall_u * cross_l * inv_det
     coef[7] = wall_u * keep_l * inv_det
 
-    def span(ref, *index):
-        return ref.at[index]
-
-    def zcopy(j, step):
-        dest = lax.rem(base + lax.rem(j, 2) + 2 * step, n_ax)
+    def zcopy(dest, u, j, f0, nf):
         slot = lax.rem(me - dest + n_ax, n_ax)
         pick = jnp.where(me < dest, 0, 1)
         return pltpu.make_async_remote_copy(
-            src_ref=ps.at[pick, :, tile(j), :], dst_ref=zrecv.at[slot, :, tile(j), :],
-            send_sem=zsend.at[j], recv_sem=zrecv_sem.at[j],
+            src_ref=ps.at[pick, pl.ds(f0, nf), tile(j), :],
+            dst_ref=zrecv.at[slot, pl.ds(f0, nf), tile(j), :],
+            send_sem=zsend.at[u], recv_sem=zrecv_sem.at[u],
             device_id=(i, dest, c), device_id_type=MESH)
+
+    def each_target(unit, direct, act):
+        if direct:
+            for step in range(1, n_ax):
+                act(zcopy(lax.rem(me + step, n_ax), *unit))
+            return
+        first = base + lax.rem(unit[0], 2)
+
+        @pl.when(first != me)
+        def _():
+            act(zcopy(first, *unit))
+
+        for step in range(1, n_ax // 2):
+            act(zcopy(lax.rem(first + 2 * step, n_ax), *unit))
 
     def forward_copy(j):
         return pltpu.make_async_remote_copy(
@@ -308,15 +332,23 @@
             send_sem=fsend.at[j], recv_sem=frecv.at[j],
             device_id=(i, sibling, c), device_id_type=MESH)
 
-    def out_copy(j):
-        return pltpu.make_async_copy(bg.at[:, :, tile(j), :], out_hbm.at[0, :, :, tile(j), :], osem.at[j])
-
-    def reduce_chunk(j):
-        at = tile(j)
+    def out_copy(u, j, f0, nf):
+        return pltpu.make_async_copy(
+            bg.at[pl.ds(f0, nf), :, tile(j), :], out_hbm.at[0, pl.ds(f0, nf), :, tile(j), :], osem.at[u])
+
+    def each_field(unit, act):
+        def body(f, carry):
+            act(f)
+            return carry
+
+        lax.fori_loop(unit[2], unit[2] + unit[3], body, 0)
+
+    def reduce_unit(unit, direct):
+        at = tile(unit[1])
         for k in range(1, n_inst):
-            ycopy(k, j).wait_recv()
-
-        def one_field(f, carry):
+            ycopy(k, *unit).wait_recv()
+
+        def one_field(f):
             running = None
             values = []
             for a in range(rows):
@@ -333,81 +365,102 @@
                 bg[f, a, at, :] = solved
             ps[0, f, at, :] = coef[0, at, :] * values[-1] + coef[1, at, :] * solved
             ps[1, f, at, :] = coef[2, at, :] * solved + coef[3, at, :] * values[-1]
-            return carry
-
-        lax.fori_loop(0, fields, one_field, 0)
-
-        @pl.when(core != lax.rem(j, 2))
-        def _():
-            zcopy(j, 0).start()
-
-        for step in range(1, n_ax // 2):
-            zcopy(j, step).start()
-
-    def gather_chunk(j):
-        at = tile(j)
-
-        @pl.when(core == lax.rem(j, 2))
-        def _():
-            landed = zrecv.at[pl.ds(1, n_ax - 1), :, at, :]
-            pltpu.make_async_copy(landed, landed, zrecv_sem.at[j]).wait()
-
-            def one_field(f, carry):
-                down = jnp.zeros((TILE, radial), jnp.float32)
-                up = jnp.zeros((TILE, radial), jnp.float32)
-                for slot in range(1, n_ax):
-                    source = lax.rem(me + slot, n_ax)
-                    value = zrecv[slot, f, at, :]
-                    down = down + jnp.where(source < base, value, 0.0)
-                    up = up + jnp.where(source > base + 1, value, 0.0)
+
+        each_field(unit, one_field)
+        each_target(unit, direct, lambda copy: copy.start())
+
+    def landed(unit):
+        block = zrecv.at[pl.ds(1, n_ax - 1), pl.ds(unit[2], unit[3]), tile(unit[1]), :]
+        pltpu.make_async_copy(block, block, zrecv_sem.at[unit[0]]).wait()
+
+    def sums(f, at, lower, upper):
+        down = jnp.zeros((TILE, radial), jnp.float32)
+        up = jnp.zeros((TILE, radial), jnp.float32)
+        for slot in range(1, n_ax):
+            source = lax.rem(me + slot, n_ax)
+            value = zrecv[slot, f, at, :]
+            down = down + jnp.where(source < lower, value, 0.0)
+            up = up + jnp.where(source > upper, value, 0.0)
+        return down, up
+
+    def gather_unit(unit):
+        at = tile(unit[1])
+
+        @pl.when(core == lax.rem(unit[0], 2))
+        def _():
+            landed(unit)
+
+            def one_field(f):
+                down, up = sums(f, at, base, base + 1)
                 beside = jnp.where(core == 0, zrecv[1, f, at, :], zrecv[n_ax - 1, f, at, :])
                 ag_out[0, f, at, :] = down + jnp.where(core == 0, ps[0, f, at, :], 0.0)
                 ag_out[1, f, at, :] = up + jnp.where(core == 0, 0.0, ps[1, f, at, :])
                 ag_in[0, f, at, :] = down + jnp.where(core == 0, 0.0, beside)
                 ag_in[1, f, at, :] = up + jnp.where(core == 0, beside, 0.0)
-                return carry
-
-            lax.fori_loop(0, fields, one_field, 0)
-            forward_copy(j).start()
-
-    def finish_chunk(j):
-        at = tile(j)
-
-        @pl.when(core != lax.rem(j, 2))
-        def _():
-            forward_copy(j).wait_recv()
-
-        def one_field(f, carry):
-            low = chain_in[0, 1, at, :] * ag_in[0, f, at, :]
-            high = chain_in[1, 1, at, :] * ag_in[1, f, at, :]
+
+            each_field(unit, one_field)
+            forward_copy(unit[0]).start()
+
+    def finish_unit(unit, direct):
+        at = tile(unit[1])
+        if direct:
+            landed(unit)
+        else:
+            @pl.when(core != lax.rem(unit[0], 2))
+            def _():
+                forward_copy(unit[0]).wait_recv()
+
+        def one_field(f):
+            low, high = sums(f, at, me, me) if direct else (ag_in[0, f, at, :], ag_in[1, f, at, :])
+            low = chain_in[0, 1, at, :] * low
+            high = chain_in[1, 1, at, :] * high
             first = bg[f, 0, at, :] + low * phi[0, at, :] + high * psi[0, at, :]
             final = bg[f, last, at, :] + low * phi[last, at, :] + high * psi[last, at, :]
             low = low + coef[4, at, :] * first + coef[5, at, :] * final
             high = high + coef[6, at, :] * first + coef[7, at, :] * final
             for a in range(rows):
                 delta = bg[f, a, at, :] + low * phi[a, at, :] + high * psi[a, at, :]
-                bg[f, a, at, :] = pad[f, a, tile(j + 1), :] + delta
-            return carry
-
-        lax.fori_loop(0, fields, one_field, 0)
-        out_copy(j).start()
+                bg[f, a, at, :] = pad[f, a, tile(unit[1] + 1), :] + delta
+
+        each_field(unit, one_field)
+        out_copy(*unit).start()
+
+    whole = chunks - 1
+    pieces = [(u, *units[u]) for u in range(whole, len(units))]
+
+    def entire(j):
+        return (j, j, 0, fields)
 
     def step(j, carry):
-        @pl.when(j < chunks)
-        def _():
-            reduce_chunk(j)
-
-        @pl.when(jnp.logical_and(j >= 1, j <= chunks))
-        def _():
-            gather_chunk(j - 1)
+        reduce_unit(entire(j), False)
+
+        @pl.when(j >= 1)
+        def _():
+            gather_unit(entire(j - 1))
 
         @pl.when(j >= 2)
         def _():
-            finish_chunk(j - 2)
+            finish_unit(entire(j - 2), False)
 
         return carry
 
-    lax.fori_loop(0, chunks + 2, step, 0)
+    lax.fori_loop(0, whole, step, 0)
+    tasks = []
+    if whole >= 2:
+        tasks.append(lambda: finish_unit(entire(whole - 2), False))
+    if whole >= 1:
+        tasks.insert(0, lambda: gather_unit(entire(whole - 1)))
+        tasks.append(lambda: finish_unit(entire(whole - 1), False))
+    if tasks:
+        tasks.pop(0)()
+    for piece in pieces:
+        reduce_unit(piece, True)
+        if tasks:
+            tasks.pop(0)()
+    for task in tasks:
+        task()
+    for piece in pieces:
+        finish_unit(piece, True)
 
     for copy in halos:
         copy.wait_send()
@@ -420,32 +473,30 @@
     def _():
         down_copy.wait_send()
 
+    def settle(unit, direct):
+        for k in range(1, n_inst):
+            ycopy(k, *unit).wait_send()
+        each_target(unit, direct, lambda copy: copy.wait_send())
+        if not direct:
+            @pl.when(core == lax.rem(unit[0], 2))
+            def _():
+                forward_copy(unit[0]).wait_send()
+        out_copy(*unit).wait()
+
     def drain(j, carry):
-        for k in range(1, n_inst):
-            ycopy(k, j).wait_send()
-
-        @pl.when(core != lax.rem(j, 2))
-        def _():
-            zcopy(j, 0).wait_send()
-
-        for s in range(1, n_ax // 2):
-            zcopy(j, s).wait_send()
-
-        @pl.when(core == lax.rem(j, 2))
-        def _():
-            forward_copy(j).wait_send()
-
-        out_copy(j).wait()
+        settle(entire(j), False)
         return carry
 
-    lax.fori_loop(0, chunks, drain, 0)
+    lax.fori_loop(0, whole, drain, 0)
+    for piece in pieces:
+        settle(piece, True)
 
 
 def local(mesh_shape, flow_state, thinc_flags):
     n_inst, n_ax, n_circ = mesh_shape["inst"], mesh_shape["ax"], mesh_shape["circ"]
     _, fields, rows, width, radial = flow_state.shape
     chunks = width // TILE
-    flags = jnp.broadcast_to(thinc_flags[0].astype(jnp.float32)[:, :, None], (rows, width, radial))
+    n_units = chunks - 1 + len(PIECES)
     f32 = jnp.float32
     scratch = [
         pltpu.VMEM((fields, rows, width + 2 * TILE, radial), f32),
@@ -457,6 +508,7 @@
         pltpu.VMEM((rows, width, radial), f32),
         pltpu.VMEM((rows, width, radial), f32),
         pltpu.VMEM((n_inst - 1, fields, rows, width, radial), f32),
+        pltpu.VMEM((rows, width, radial), f32),
         pltpu.VMEM((2, fields + 2, rows, radial), f32),
         pltpu.VMEM((2, fields + 2, rows, radial), f32),
         pltpu.VMEM((2, 2, width, radial), f32),
@@ -467,17 +519,17 @@
         pltpu.VMEM((2, fields, width, radial), f32),
         pltpu.VMEM((2, fields, width, radial), f32),
         pltpu.SemaphoreType.DMA,
-        pltpu.SemaphoreType.DMA((n_inst - 1, chunks)),
-        pltpu.SemaphoreType.DMA((n_inst - 1, chunks)),
+        pltpu.SemaphoreType.DMA((n_inst - 1, n_units)),
+        pltpu.SemaphoreType.DMA((n_inst - 1, n_units)),
         pltpu.SemaphoreType.DMA((2,)),
         pltpu.SemaphoreType.DMA((2,)),
         pltpu.SemaphoreType.DMA((2,)),
         pltpu.SemaphoreType.DMA((2,)),
-        pltpu.SemaphoreType.DMA((chunks,)),
-        pltpu.SemaphoreType.DMA((chunks,)),
-        pltpu.SemaphoreType.DMA((chunks,)),
-        pltpu.SemaphoreType.DMA((chunks,)),
-        pltpu.SemaphoreType.DMA((chunks,)),
+        pltpu.SemaphoreType.DMA((n_units,)),
+        pltpu.SemaphoreType.DMA((n_units,)),
+        pltpu.SemaphoreType.DMA((n_units,)),
+        pltpu.SemaphoreType.DMA((n_units,)),
+        pltpu.SemaphoreType.DMA((n_units,)),
     ]
     return pl.pallas_call(
         functools.partial(
@@ -488,9 +540,9 @@
         out_specs=pl.BlockSpec(memory_space=pl.ANY),
         scratch_shapes=scratch,
         compiler_params=pltpu.CompilerParams(
-            collective_id=0, has_side_effects=True, vmem_limit_bytes=48 * 1024 * 1024
+            collective_id=0, has_side_effects=True, vmem_limit_bytes=60 * 1024 * 1024
         ),
-    )(flow_state, flags)
+    )(flow_state, thinc_flags)
 
 
 def solution(mesh):

time: 55.7 us -> 58.3 us (1.047)
  Pallas kernels: 52 us -> 55.2 us
  other arithmetic: 0.69 us -> 0 us
    pallas_call x1, Pallas kernels: 52 us -> 55.2 us  [local(): pl.pallas_call(functools.partial(kernel, (n_inst, n_ax, n_circ, rows, wid...]
    convert_element_type x1 -> x0, other arithmetic: 0.69 us -> none  [local(): thinc_flags[0].astype(jnp.float32)[:, :, None]]
    unnamed x3 -> x1, local copies, waits for them, and re-layouts: 2.73 us -> 2.94 us
where the time goes in v2:
time: 58.3 us; the launch traced here: 58.1 us
  Pallas kernels  55.2 us (95%)
  local copies, waits for them, and re-layouts  2.94 us (5%)
    pallas_call x1, Pallas kernels, local(): pl.pallas_call(functools.partial(kernel, (n_inst, n_ax, n_circ, rows, wid...  55.2 us
    unnamed x1, local copies, waits for them, and re-layouts  2.94 us

profile of v2, /device:TPU:0, one launch (start us, length us, event | category | flops | bytes accessed | tf_op | source)
XLA Modules:
  0.0 58.1 jit_solution(2091574069153315949)
XLA Ops:
  0.0 55.2 %shard_map.28 = f32[1,7,8,64,128]{4,3,2,1,0:T(8,128)} custom-call(f32[1,7,8,64,128]{4,3,2,1,0:T(8,128)} %q_hbm.1, s32[1,8,64]{2,1,0:T(8,128)} %flag_ref.1), custom_call_target="tpu_custom_call" | custom-call | tf_op jit(solution)/shard_map/pallas_call | solution.py:534
  55.2 2.9 %copy.4 = f32[1,7,8,64,128]{4,3,2,1,0:T(8,128)} copy(f32[1,7,8,64,128]{4,3,2,1,0:T(8,128)} %shard_map.28) | data formatting | bytes 3670016

commit v3 on v2

--- a/solution.py
+++ b/solution.py
@@ -61,8 +61,8 @@
 
 
 def kernel(sizes, weights, q_hbm, flag_ref, out_hbm, pad, prim, flux, bg, iv, piv, phi, psi, rem, flag_wide,
-           halo_out, halo_in, chain_out, chain_in, coef, ps, zrecv, ag_out, ag_in,
-           load_sem, ysend, yrecv, hsend, hrecv, csend, crecv, zsend, zrecv_sem, fsend, frecv, osem):
+           halo_out, halo_in, line_out, line_in, back_out, chain_in, coef, ps, zrecv, ag_out, ag_in,
+           load_sem, ysend, yrecv, hsend, hrecv, csend, crecv, bsend, brecv, zsend, zrecv_sem, fsend, frecv, osem):
     n_inst, n_ax, n_circ, rows, width, radial = sizes
     fields = 7
     chunks = width // TILE
@@ -158,68 +158,53 @@
     lax.fori_loop(0, chunks, own_tile, 0)
 
     last = rows - 1
-
-    def chain_copy(side, target):
+    line_out[0] = phi[0]
+    line_out[1] = phi[last]
+    line_out[2] = psi[last]
+
+    def owner(j):
+        return (j * n_ax) // chunks
+
+    def slot_of(device, target):
+        return lax.rem(device - target + n_ax, n_ax)
+
+    def line_copy(j):
         return pltpu.make_async_remote_copy(
-            src_ref=chain_out.at[side], dst_ref=chain_in.at[side], send_sem=csend.at[side],
-            recv_sem=crecv.at[side], device_id=(i, target, c), device_id_type=MESH)
-
-    up_copy = chain_copy(0, jnp.minimum(me + 1, n_ax - 1))
-    down_copy = chain_copy(1, jnp.maximum(me - 1, 0))
-
-    def chain_up():
-        @pl.when(me == 0)
-        def _():
-            chain_in[0, 0] = jnp.zeros((width, radial), jnp.float32)
-            chain_in[0, 1] = jnp.ones((width, radial), jnp.float32)
-
-        @pl.when(me > 0)
-        def _():
-            up_copy.wait_recv()
-
-        wall, scale = chain_in[0, 0], chain_in[0, 1]
-        den = 1.0 / (1.0 - wall * phi[0])
-        mix = phi[last] * wall * den
-        following = scale * phi[last] * den
-        chain_out[0, 0] = psi[last] + mix * psi[0]
-        chain_out[0, 1] = following
-
-        @pl.when(me < n_ax - 1)
-        def _():
-            up_copy.start()
-
-        inverse = 1.0 / following
-        coef[0] = inverse
-        coef[1] = mix * inverse
-
-    def chain_down():
-        @pl.when(me == n_ax - 1)
-        def _():
-            chain_in[1, 0] = jnp.zeros((width, radial), jnp.float32)
-            chain_in[1, 1] = jnp.ones((width, radial), jnp.float32)
-
-        @pl.when(me < n_ax - 1)
-        def _():
-            down_copy.wait_recv()
-
-        wall, scale = chain_in[1, 0], chain_in[1, 1]
-        den = 1.0 / (1.0 - wall * psi[last])
-        mix = psi[0] * wall * den
-        following = scale * psi[0] * den
-        chain_out[1, 0] = phi[0] + mix * phi[last]
-        chain_out[1, 1] = following
-
-        @pl.when(me > 0)
-        def _():
-            down_copy.start()
-
-        inverse = 1.0 / following
-        coef[2] = inverse
-        coef[3] = mix * inverse
-
-    lower_half = me < n_ax // 2
-    pl.when(lower_half)(chain_up)
-    pl.when(jnp.logical_not(lower_half))(chain_down)
+            src_ref=line_out.at[:, tile(j), :], dst_ref=line_in.at[slot_of(me, owner(j)), :, tile(j), :],
+            send_sem=csend.at[j], recv_sem=crecv.at[j],
+            device_id=(i, owner(j), c), device_id_type=MESH)
+
+    def back_copy(j, target):
+        return pltpu.make_async_remote_copy(
+            src_ref=back_out.at[slot_of(target, owner(j)), :, tile(j), :], dst_ref=chain_in.at[:, tile(j), :],
+            send_sem=bsend.at[j], recv_sem=brecv.at[j],
+            device_id=(i, target, c), device_id_type=MESH)
+
+    def hand_over(j):
+        line_in[0, :, tile(j), :] = line_out[:, tile(j), :]
+
+    for j in range(chunks):
+        pl.when(me != owner(j))(lambda j=j: line_copy(j).start())
+        pl.when(me == owner(j))(lambda j=j: hand_over(j))
+
+    def own_lines(j):
+        at = tile(j)
+        block_in = line_in.at[pl.ds(1, n_ax - 1), :, at, :]
+        pltpu.make_async_copy(block_in, block_in, crecv.at[j]).wait()
+        for side in range(2):
+            wall = jnp.zeros((TILE, radial), jnp.float32)
+            scale = jnp.ones((TILE, radial), jnp.float32)
+            for device in range(n_ax) if side == 0 else reversed(range(n_ax)):
+                slot = slot_of(device, owner(j))
+                back_out[slot, 2 * side, at, :] = wall
+                back_out[slot, 2 * side + 1, at, :] = scale
+                near, across, far = (line_in[slot, n, at, :] for n in ((0, 1, 2), (2, 1, 0))[side])
+                factor = across / (1.0 - wall * near)
+                scale = scale * factor
+                wall = far + wall * factor * across
+        chain_in[:, at, :] = back_out[0, :, at, :]
+        for step in range(1, n_ax):
+            back_copy(j, lax.rem(me + step, n_ax)).start()
 
     for copy in halos:
         copy.wait_recv()
@@ -239,6 +224,9 @@
             prim[0, a, pl.ds(t * TILE, TILE), :] = vel_circ
             prim[1, a, pl.ds(t * TILE, TILE), :] = pressure
             prim[2, a, pl.ds(t * TILE, TILE), :] = jnp.abs(vel_circ) + sound
+
+    for j in range(chunks):
+        pl.when(me == owner(j))(lambda j=j: own_lines(j))
 
     def behind(low, mid, by):
         return jnp.where(sub < by, pltpu.roll(low, by, 0), pltpu.roll(mid, by, 0))
@@ -291,10 +279,13 @@
 
     lax.fori_loop(0, chunks, right_side, 0)
 
-    pl.when(lower_half)(chain_down)
-    pl.when(jnp.logical_not(lower_half))(chain_up)
-
-    wall_l, wall_u = chain_in[0, 0], chain_in[1, 0]
+    for j in range(chunks):
+        pl.when(me != owner(j))(lambda j=j: back_copy(j, me).wait_recv())
+
+    wall_l, scale_l, wall_u, scale_u = (chain_in[n] for n in range(4))
+    for n, wall, scale, near in ((0, wall_l, scale_l, phi[0]), (2, wall_u, scale_u, psi[last])):
+        coef[n] = (1.0 - wall * near) / (scale * phi[last])
+        coef[n + 1] = wall / scale
     keep_l, keep_u = 1.0 - wall_l * phi[0], 1.0 - wall_u * psi[last]
     cross_l, cross_u = wall_l * phi[last], wall_u * psi[0]
     inv_det = 1.0 / (keep_l * keep_u - cross_l * cross_u)
@@ -341,7 +332,7 @@
             act(f)
             return carry
 
-        lax.fori_loop(unit[2], unit[2] + unit[3], body, 0)
+        lax.fori_loop(unit[2], unit[2] + unit[3], body, 0, unroll=True)
 
     def reduce_unit(unit, direct):
         at = tile(unit[1])
@@ -412,8 +403,8 @@
 
         def one_field(f):
             low, high = sums(f, at, me, me) if direct else (ag_in[0, f, at, :], ag_in[1, f, at, :])
-            low = chain_in[0, 1, at, :] * low
-            high = chain_in[1, 1, at, :] * high
+            low = chain_in[1, at, :] * low
+            high = chain_in[3, at, :] * high
             first = bg[f, 0, at, :] + low * phi[0, at, :] + high * psi[0, at, :]
             final = bg[f, last, at, :] + low * phi[last, at, :] + high * psi[last, at, :]
             low = low + coef[4, at, :] * first + coef[5, at, :] * final
@@ -432,46 +423,45 @@
         return (j, j, 0, fields)
 
     def step(j, carry):
-        reduce_unit(entire(j), False)
-
-        @pl.when(j >= 1)
-        def _():
-            gather_unit(entire(j - 1))
-
         @pl.when(j >= 2)
         def _():
-            finish_unit(entire(j - 2), False)
-
+            gather_unit(entire(j - 2))
+
+        @pl.when(j >= 3)
+        def _():
+            finish_unit(entire(j - 3), False)
+
+        reduce_unit(entire(j), False)
         return carry
 
     lax.fori_loop(0, whole, step, 0)
-    tasks = []
-    if whole >= 2:
-        tasks.append(lambda: finish_unit(entire(whole - 2), False))
-    if whole >= 1:
-        tasks.insert(0, lambda: gather_unit(entire(whole - 1)))
-        tasks.append(lambda: finish_unit(entire(whole - 1), False))
-    if tasks:
-        tasks.pop(0)()
-    for piece in pieces:
+
+    def late(act, j, *rest):
+        if j >= 0:
+            act(entire(j), *rest)
+
+    late(gather_unit, whole - 2)
+    late(finish_unit, whole - 3, False)
+    for n, piece in enumerate(pieces):
         reduce_unit(piece, True)
-        if tasks:
-            tasks.pop(0)()
-    for task in tasks:
-        task()
+        if n == 0:
+            late(gather_unit, whole - 1)
+            late(finish_unit, whole - 2, False)
+        if n == min(1, len(pieces) - 1):
+            late(finish_unit, whole - 1, False)
     for piece in pieces:
         finish_unit(piece, True)
 
     for copy in halos:
         copy.wait_send()
 
-    @pl.when(me < n_ax - 1)
-    def _():
-        up_copy.wait_send()
-
-    @pl.when(me > 0)
-    def _():
-        down_copy.wait_send()
+    def settle_lines(j):
+        for step in range(1, n_ax):
+            back_copy(j, lax.rem(me + step, n_ax)).wait_send()
+
+    for j in range(chunks):
+        pl.when(me != owner(j))(lambda j=j: line_copy(j).wait_send())
+        pl.when(me == owner(j))(lambda j=j: settle_lines(j))
 
     def settle(unit, direct):
         for k in range(1, n_inst):
@@ -511,8 +501,10 @@
         pltpu.VMEM((rows, width, radial), f32),
         pltpu.VMEM((2, fields + 2, rows, radial), f32),
         pltpu.VMEM((2, fields + 2, rows, radial), f32),
-        pltpu.VMEM((2, 2, width, radial), f32),
-        pltpu.VMEM((2, 2, width, radial), f32),
+        pltpu.VMEM((3, width, radial), f32),
+        pltpu.VMEM((n_ax, 3, width, radial), f32),
+        pltpu.VMEM((n_ax, 4, width, radial), f32),
+        pltpu.VMEM((4, width, radial), f32),
         pltpu.VMEM((8, width, radial), f32),
         pltpu.VMEM((2, fields, width, radial), f32),
         pltpu.VMEM((n_ax, fields, width, radial), f32),
@@ -523,8 +515,10 @@
         pltpu.SemaphoreType.DMA((n_inst - 1, n_units)),
         pltpu.SemaphoreType.DMA((2,)),
         pltpu.SemaphoreType.DMA((2,)),
-        pltpu.SemaphoreType.DMA((2,)),
-        pltpu.SemaphoreType.DMA((2,)),
+        pltpu.SemaphoreType.DMA((chunks,)),
+        pltpu.SemaphoreType.DMA((chunks,)),
+        pltpu.SemaphoreType.DMA((chunks,)),
+        pltpu.SemaphoreType.DMA((chunks,)),
         pltpu.SemaphoreType.DMA((n_units,)),
         pltpu.SemaphoreType.DMA((n_units,)),
         pltpu.SemaphoreType.DMA((n_units,)),
@@ -540,7 +534,7 @@
         out_specs=pl.BlockSpec(memory_space=pl.ANY),
         scratch_shapes=scratch,
         compiler_params=pltpu.CompilerParams(
-            collective_id=0, has_side_effects=True, vmem_limit_bytes=60 * 1024 * 1024
+            collective_id=0, has_side_effects=True, vmem_limit_bytes=52 * 1024 * 1024
         ),
     )(flow_state, thinc_flags)
 

time: 58.3 us -> 54.9 us (0.942)
  Pallas kernels: 55.2 us -> 52.8 us
  local copies, waits for them, and re-layouts: 2.94 us -> 1.92 us
    pallas_call x1, Pallas kernels: 55.2 us -> 52.8 us  [local(): pl.pallas_call(functools.partial(kernel, (n_inst, n_ax, n_circ, rows, wid...]
    unnamed x1 -> x3, local copies, waits for them, and re-layouts: 2.94 us -> 1.92 us
where the time goes in v3:
time: 54.9 us; the launch traced here: 54.7 us
  Pallas kernels  52.8 us (96%)
  local copies, waits for them, and re-layouts  1.92 us (3%)
    pallas_call x1, Pallas kernels, local(): pl.pallas_call(functools.partial(kernel, (n_inst, n_ax, n_circ, rows, wid...  52.8 us
    unnamed x3, local copies, waits for them, and re-layouts  1.92 us

profile of v3, /device:TPU:0, one launch (start us, length us, event | category | flops | bytes accessed | tf_op | source)
XLA Modules:
  0.0 54.7 jit_solution(9576743220141461684)
XLA Ops:
  0.0 0.0 copy-start
  0.0 0.7 %copy-done = s32[1,8,64]{2,1,0:T(8,128)S(1)} copy-done((s32[1,8,64]{2,1,0:T(8,128)S(1)}, s32[1,8,64]{2,1,0:T(8,128)}, u32[]{:S(2)}) %copy-start) | copy-done | bytes 2072
  0.7 52.8 %shard_map.28 = f32[1,7,8,64,128]{4,3,2,1,0:T(8,128)S(1)} custom-call(f32[1,7,8,64,128]{4,3,2,1,0:T(8,128)} %q_hbm.1, s32[1,8,64]{2,1,0:T(8,128)S(1)} %copy-done), custom_call_target="tpu_custom_call" | custom-call | tf_op jit(solution)/shard_map/pallas_call | solution.py:528
  53.5 1.2 %copy.4 = f32[1,7,8,64,128]{4,3,2,1,0:T(8,128)} copy(f32[1,7,8,64,128]{4,3,2,1,0:T(8,128)S(1)} %shard_map.28) | data formatting | bytes 3670016
Async XLA Ops:
  0.0 0.7 %copy-start = (s32[1,8,64]{2,1,0:T(8,128)S(1)}, s32[1,8,64]{2,1,0:T(8,128)}, u32[]{:S(2)}) copy-start(s32[1,8,64]{2,1,0:T(8,128)} %flag_ref.1) | copy-start | bytes 6148
